TPU v7x, 256 devices: a whole 4x4x8 slice. The times are simulated.
256 devices in a mesh: grp: 8 (over z), seq: 32 (over x, y, core).
Axes of the slice: x: 4, y: 4, z: 8, core: 2. Of those that a mesh axis runs over, the one named last changes fastest.
Arguments:
- queries: bfloat16 [8, 1024, 4096], P('grp', 'seq'), may hold values from -96 to 96
- attn_keys: bfloat16 [8, 1024, 4096], P('grp', 'seq'), may hold values from -4 to 4
- attn_values: bfloat16 [8, 1024, 4096], P('grp', 'seq'), may hold values from -6 to 6
- byte_grads: bfloat16 [8, 8192, 4096], P('grp', 'seq'), may hold values from -6 to 6
- seg_starts: int32 [8, 32, 32], P('grp', 'seq'), may hold values from 0 to 256, as said below
- up_gain: float32 [4096], replicated, may hold values from 0.1 to 1.9
Outputs:
- grad_queries: bfloat16 [8, 1024, 4096], P('grp', 'seq')
- grad_keys: bfloat16 [8, 1024, 4096], P('grp', 'seq')
- grad_values: bfloat16 [8, 1024, 4096], P('grp', 'seq')
- grad_gain: float32 [4096], P('seq')
Inputs may be any that keep to these rules, and one draw needn't show every extreme that they name: `seg_starts`: in every row each shard's entries rise strictly, the used ones below 256 and the unused slots after them equal to 256; every shard starts at least 8 segments and some shard of every row exactly 32; shard 0's first entry is 0.
All inputs are finite; a program needn't handle non-finite values.
Results may differ from a plain program's by a relative error of at most 0.012.
Values may be sent and summed in bfloat16 or wider, within the bound.
No kernel may reach another device: no remote copies, remote signals or barrier semaphores. Data moves between devices by JAX's collectives and lax.ppermute only.
A program may use at most 64 MiB of HBM per device.

v0:
```python
import math
import jax
import jax.numpy as jnp
from jax import lax
from jax.sharding import PartitionSpec as P

HD = 128


def shifted(value, axis, by):
    devices = lax.axis_size(axis)
    pairs = [(i, i + by) for i in range(devices) if 0 <= i + by < devices]
    return lax.ppermute(value, axis, pairs)


def shortened(value):
    return jax.tree.map(lambda a: a.astype(jnp.bfloat16) if a.dtype == jnp.float32 else a, value)


def head_grads(query_head, key_head, value_head, upstream, key_valid):
    seq_rows = query_head.shape[0]
    head_width = query_head.shape[1]
    block_rows = math.gcd(seq_rows, 512)
    block_total = seq_rows // block_rows
    scaling = 1.0 / math.sqrt(head_width)
    key_total = jnp.zeros((seq_rows, head_width), jnp.float32)
    value_total = jnp.zeros((seq_rows, head_width), jnp.float32)
    query_parts = []
    output_parts = []
    for block_index in range(block_total):
        first_row = block_index * block_rows
        prefix = first_row + block_rows
        query_block = query_head[first_row:prefix]
        upstream_block = upstream[first_row:prefix]
        key_prefix = key_head[:prefix]
        value_prefix = value_head[:prefix]
        scores = (
            jnp.einsum("qd,kd->qk", query_block, key_prefix, preferred_element_type=jnp.float32)
            * scaling
        )
        row_ids = first_row + jnp.arange(block_rows, dtype=jnp.int32)[:, None]
        col_ids = jnp.arange(prefix, dtype=jnp.int32)[None, :]
        allowed = (col_ids <= row_ids) & key_valid[None, :prefix]
        scores = jnp.where(allowed, scores, -1e30)
        row_max = jnp.max(scores, axis=1, keepdims=True)
        weights = jnp.exp(scores - row_max)
        attn_probs = weights / jnp.sum(weights, axis=1, keepdims=True)
        probs_low = attn_probs.astype(jnp.bfloat16)
        attn_out = jnp.einsum(
            "qk,kd->qd", probs_low, value_prefix, preferred_element_type=jnp.float32
        ).astype(jnp.bfloat16)
        grad_probs = jnp.einsum(
            "qd,kd->qk", upstream_block, value_prefix, preferred_element_type=jnp.float32
        )
        row_delta = jnp.sum(
            upstream_block.astype(jnp.float32) * attn_out.astype(jnp.float32), axis=1, keepdims=True
        )
        grad_scores = (attn_probs * (grad_probs - row_delta)).astype(jnp.bfloat16)
        grad_query = (
            jnp.einsum("qk,kd->qd", grad_scores, key_prefix, preferred_element_type=jnp.float32)
            * scaling
        ).astype(jnp.bfloat16)
        key_total = key_total.at[:prefix].add(
            jnp.einsum("qk,qd->kd", grad_scores, query_block, preferred_element_type=jnp.float32)
        )
        value_total = value_total.at[:prefix].add(
            jnp.einsum("qk,qd->kd", probs_low, upstream_block, preferred_element_type=jnp.float32)
        )
        query_parts.append(grad_query)
        output_parts.append(attn_out)
    grad_query = jnp.concatenate(query_parts, axis=0)
    attn_out = jnp.concatenate(output_parts, axis=0)
    grad_key = (key_total * scaling).astype(jnp.bfloat16)
    grad_value = value_total.astype(jnp.bfloat16)
    return (grad_query, grad_key, grad_value, attn_out)


def pool_bytes(byte_grads, seg_starts, slot_count):
    byte_count = byte_grads.shape[1]
    local_starts = seg_starts[0, 0]
    filled = jnp.sum((local_starts < byte_count).astype(jnp.int32))
    position = jnp.arange(byte_count, dtype=jnp.int32)
    started = jnp.sum((local_starts[None, :] <= position[:, None]).astype(jnp.int32), axis=1)
    slot_ids = jnp.arange(slot_count, dtype=jnp.int32)
    member = (started[None, :] - 1 == slot_ids[:, None]).astype(jnp.bfloat16)
    byte_rows = byte_grads[0]
    own_sums = jnp.dot(member, byte_rows, preferred_element_type=jnp.float32)
    leading = (started == 0).astype(jnp.bfloat16)[None, :]
    carried = jnp.dot(leading, byte_rows, preferred_element_type=jnp.float32)
    incoming = shifted(carried, "seq", -1)
    is_last = (slot_ids == filled - 1)[:, None]
    pooled = own_sums + jnp.where(is_last, incoming, 0.0)
    return pooled.astype(jnp.bfloat16)


def per_device(queries, attn_keys, attn_values, byte_grads, seg_starts, up_gain):
    slot_count = queries.shape[1]
    model_width = queries.shape[2]
    byte_count = byte_grads.shape[1]
    seq_count = lax.axis_size("seq")
    shard_index = lax.axis_index("seq")
    heads_here = model_width // (seq_count * HD)
    col_count = heads_here * HD
    all_starts = lax.all_gather(seg_starts[0], "seq", axis=0, tiled=True)
    key_valid = (all_starts < byte_count).reshape(-1)

    def by_heads(tensor):
        return tensor.reshape(slot_count, seq_count * heads_here, HD)

    pooled_low = pool_bytes(byte_grads, seg_starts, slot_count)
    head_query, head_key, head_value, head_pool = (
        lax.all_to_all(by_heads(queries[0]), "seq", split_axis=1, concat_axis=0, tiled=True),
        lax.all_to_all(by_heads(attn_keys[0]), "seq", split_axis=1, concat_axis=0, tiled=True),
        lax.all_to_all(by_heads(attn_values[0]), "seq", split_axis=1, concat_axis=0, tiled=True),
        lax.all_to_all(by_heads(pooled_low), "seq", split_axis=1, concat_axis=0, tiled=True),
    )
    gain_here = lax.dynamic_slice_in_dim(up_gain, shard_index * col_count, col_count).reshape(
        1, heads_here, HD
    )
    upstream = (gain_here * head_pool.astype(jnp.float32)).astype(jnp.bfloat16)

    def per_head(head_items):
        return head_grads(head_items[0], head_items[1], head_items[2], head_items[3], key_valid)

    stacked = tuple(
        (jnp.moveaxis(operand, 1, 0) for operand in (head_query, head_key, head_value, upstream))
    )
    results = lax.map(per_head, stacked)
    grad_query, grad_key, grad_value, attn_out = tuple(
        (jnp.moveaxis(operand, 0, 1) for operand in results)
    )

    def to_seq(tensor):
        return tensor.reshape(1, slot_count, model_width)

    returned = (
        lax.all_to_all(
            shortened(grad_query), "seq", split_axis=0, concat_axis=1, tiled=True
        ).astype(grad_query.dtype),
        lax.all_to_all(grad_key, "seq", split_axis=0, concat_axis=1, tiled=True),
        lax.all_to_all(grad_value, "seq", split_axis=0, concat_axis=1, tiled=True),
        lax.all_to_all(shortened(attn_out), "seq", split_axis=0, concat_axis=1, tiled=True).astype(
            attn_out.dtype
        ),
    )
    seq_out = returned[3].reshape(slot_count, model_width)
    seq_terms = jnp.sum(seq_out.astype(jnp.float32) * pooled_low.astype(jnp.float32), axis=0)
    gain_total = lax.psum(seq_terms, ("grp", "seq"))
    grad_gain = lax.dynamic_slice_in_dim(gain_total, shard_index * col_count, col_count)
    return (to_seq(returned[0]), to_seq(returned[1]), to_seq(returned[2]), grad_gain)


def solution(mesh):
    return jax.shard_map(
        per_device,
        mesh=mesh,
        in_specs=(
            P("grp", "seq", None),
            P("grp", "seq", None),
            P("grp", "seq", None),
            P("grp", "seq", None),
            P("grp", "seq", None),
            P(),
        ),
        out_specs=(P("grp", "seq", None), P("grp", "seq", None), P("grp", "seq", None), P("seq")),
        check_vma=False,
    )
```

profile of v0, /device:TPU:1, one launch (start us, length us, event | category | flops | bytes accessed | tf_op | source)
XLA Modules:
  0.0 227.1 jit_solution(2610333382745810122)
XLA Ops:
  0.7 1.1 copy.88
  2.6 8.6 %all-to-all-start = ((bf16[32,32,128]{2,0,1:T(8,128)(2,1)}), bf16[32,32,128]{2,0,1:T(8,128)(2,1)S(1)}, u32[]{:S(2)}, u32[]{:S(2)}) async-start(bf16[32,32,128]{2,0,1:T(8,128)(2,1)} %copy.70), calls=%async_computation | async-start | bytes 524288 | tf_op jit(solution)/shard_map/all_to_all | solution.py:112
  12.4 2.1 collective-permute-start
  14.5 23.7 %all-gather = s32[32,1,32]{2,1,0:T(1,128)S(1)} all-gather(s32[1,1,32]{2,1,0:T(1,128)S(1)} %copy-done.19), channel_id=2, replica_groups=mesh['grp'=8,'seq'=32] {'seq'}, dimensions={0}, use_global_device_ids=true | all-gather | bytes 4224 | tf_op jit(solution)/shard_map/all_gather | solution.py:104
  42.8 5.8 %all-to-all-start.1 = ((bf16[32,32,128]{2,0,1:T(8,128)(2,1)}), bf16[32,32,128]{2,0,1:T(8,128)(2,1)S(1)}, u32[]{:S(2)}, u32[]{:S(2)}) async-start(bf16[32,32,128]{2,0,1:T(8,128)(2,1)} %copy.71), calls=%async_computation.1 | async-start | bytes 524288 | tf_op jit(solution)/shard_map/all_to_all | solution.py:113
  49.3 8.2 %all-to-all-done.1 = bf16[32,32,128]{2,0,1:T(8,128)(2,1)S(1)} async-done(((bf16[32,32,128]{2,0,1:T(8,128)(2,1)}), bf16[32,32,128]{2,0,1:T(8,128)(2,1)S(1)}, u32[]{:S(2)}, u32[]{:S(2)}) %all-to-all-start.1) | async-done | bytes 262176 | tf_op jit(solution)/shard_map/all_to_all | solution.py:113
  57.5 3.7 %all-to-all-start.3 = ((bf16[32,32,128]{2,0,1:T(8,128)(2,1)}), bf16[32,32,128]{2,0,1:T(8,128)(2,1)S(1)}, u32[]{:S(2)}, u32[]{:S(2)}) async-start(bf16[32,32,128]{2,0,1:T(8,128)(2,1)} %copy.73), calls=%async_computation.3 | async-start | bytes 524288 | tf_op jit(solution)/shard_map/all_to_all | solution.py:114
  63.2 1.8 fusion.5
  65.0 5.4 %all-to-all-done.3 = bf16[32,32,128]{2,0,1:T(8,128)(2,1)S(1)} async-done(((bf16[32,32,128]{2,0,1:T(8,128)(2,1)}), bf16[32,32,128]{2,0,1:T(8,128)(2,1)S(1)}, u32[]{:S(2)}, u32[]{:S(2)}) %all-to-all-start.3) | async-done | bytes 262176 | tf_op jit(solution)/shard_map/all_to_all | solution.py:114
  70.4 4.4 %all-to-all-start.2 = ((bf16[32,32,128]{2,0,1:T(8,128)(2,1)}), bf16[32,32,128]{2,0,1:T(8,128)(2,1)}, u32[]{:S(2)}, u32[]{:S(2)}) async-start(bf16[32,32,128]{2,0,1:T(8,128)(2,1)} %copy_bitcast_fusion), calls=%async_computation.2 | async-start | bytes 524288 | tf_op jit(solution)/shard_map/all_to_all | solution.py:115
  75.4 1.3 fusion.33
  76.9 1.1 convolution_convert_fusion.1
  78.9 4.9 %all-to-all-done.2 = bf16[32,32,128]{2,0,1:T(8,128)(2,1)} async-done(((bf16[32,32,128]{2,0,1:T(8,128)(2,1)}), bf16[32,32,128]{2,0,1:T(8,128)(2,1)}, u32[]{:S(2)}, u32[]{:S(2)}) %all-to-all-start.2) | async-done | bytes 262176 | tf_op jit(solution)/shard_map/all_to_all | solution.py:115
  83.9 1.0 bitcast_convert_fusion
  85.0 2.2 multiply_reduce_fusion.1
  89.5 1.1 fusion.16
  93.2 3.7 %all-to-all-start.5 = ((bf16[32,2,2048]{2,1,0:T(2,128)(2,1)}), bf16[32,2,2048]{2,1,0:T(2,128)(2,1)S(1)}, u32[]{:S(2)}, u32[]{:S(2)}) async-start(bf16[32,2,2048]{2,1,0:T(2,128)(2,1)} %reshape.259), calls=%async_computation.5 | async-start | bytes 524288 | tf_op jit(solution)/shard_map/all_to_all | solution.py:140
  98.3 1.5 reduce.16
  99.8 1.7 reshape.257
  101.5 4.5 %all-to-all-done.5 = bf16[32,2,2048]{2,1,0:T(2,128)(2,1)S(1)} async-done(((bf16[32,2,2048]{2,1,0:T(2,128)(2,1)}), bf16[32,2,2048]{2,1,0:T(2,128)(2,1)S(1)}, u32[]{:S(2)}, u32[]{:S(2)}) %all-to-all-start.5) | async-done | bytes 262176 | tf_op jit(solution)/shard_map/all_to_all | solution.py:140
  106.0 3.7 %all-to-all-start.4 = ((bf16[32,2,2048]{2,1,0:T(2,128)(2,1)}), bf16[32,2,2048]{2,1,0:T(2,128)(2,1)S(1)}, u32[]{:S(2)}, u32[]{:S(2)}) async-start(bf16[32,2,2048]{2,1,0:T(2,128)(2,1)} %reshape.257), calls=%async_computation.4 | async-start | bytes 524288 | tf_op jit(solution)/shard_map/all_to_all | solution.py:137
  109.7 1.6 maximum_bitcast_fusion.1
  111.4 2.4 %reduce.19 = bf16[1024,128]{1,0:T(8,128)(2,1)} reduce(bf16[1024,1,128]{2,0,1:T(8,128)(2,1)} %maximum_bitcast_fusion.1, bf16[]{:T(256)} %broadcast.160), dimensions={1}, to_apply=%copy.81.reduce_sub_computation | reduce | bytes 524290 | tf_op jit(solution)/shard_map/transpose | solution.py:130
  113.8 1.7 reshape.263
  115.5 3.3 %all-to-all-done.4 = bf16[32,2,2048]{2,1,0:T(2,128)(2,1)S(1)} async-done(((bf16[32,2,2048]{2,1,0:T(2,128)(2,1)}), bf16[32,2,2048]{2,1,0:T(2,128)(2,1)S(1)}, u32[]{:S(2)}, u32[]{:S(2)}) %all-to-all-start.4) | async-done | bytes 262176 | tf_op jit(solution)/shard_map/all_to_all | solution.py:137
  118.8 4.4 %all-to-all-start.7 = ((bf16[32,2,2048]{2,1,0:T(2,128)(2,1)}), bf16[32,2,2048]{2,1,0:T(2,128)(2,1)}, u32[]{:S(2)}, u32[]{:S(2)}) async-start(bf16[32,2,2048]{2,1,0:T(2,128)(2,1)} %reshape.263), calls=%async_computation.7 | async-start | bytes 524288 | tf_op jit(solution)/shard_map/all_to_all | solution.py:142
  123.5 2.1 fusion.14
  127.2 5.1 %all-to-all-done.7 = bf16[32,2,2048]{2,1,0:T(2,128)(2,1)} async-done(((bf16[32,2,2048]{2,1,0:T(2,128)(2,1)}), bf16[32,2,2048]{2,1,0:T(2,128)(2,1)}, u32[]{:S(2)}, u32[]{:S(2)}) %all-to-all-start.7) | async-done | bytes 262176 | tf_op jit(solution)/shard_map/all_to_all | solution.py:142
  132.3 4.6 %all-to-all-start.6 = ((bf16[32,2,2048]{2,1,0:T(2,128)(2,1)}), bf16[32,2,2048]{2,1,0:T(2,128)(2,1)}, u32[]{:S(2)}, u32[]{:S(2)}) async-start(bf16[32,2,2048]{2,1,0:T(2,128)(2,1)} %reshape.261), calls=%async_computation.6 | async-start | bytes 524288 | tf_op jit(solution)/shard_map/all_to_all | solution.py:141
  139.4 2.2 reshape.264
  142.8 80.6 %psum.7 = f32[4096]{0:T(1024)S(1)} all-reduce(f32[4096]{0:T(1024)S(1)} %fusion.20), channel_id=1, replica_groups=mesh['grp'=8,'seq'=32] {'grp','seq'}, use_global_device_ids=true, to_apply=%region_9.10 | all-reduce | flops 4096 | bytes 32768 | tf_op jit(solution)/shard_map/psum | solution.py:148
  224.0 2.2 reshape.262
  (98 shorter events, 23.6 us)
Async XLA Ops:
  0.6 11.4 %copy-start = (bf16[1,256,4096]{2,1,0:T(8,128)(2,1)S(1)}, bf16[1,256,4096]{2,1,0:T(8,128)(2,1)}, u32[]{:S(2)}) copy-start(bf16[1,256,4096]{2,1,0:T(8,128)(2,1)} %param.21) | copy-start | bytes 6291460
  0.6 13.9 %copy-start.19 = (s32[1,1,32]{2,1,0:T(1,128)S(1)}, s32[1,1,32]{2,1,0:T(1,128)}, u32[]{:S(2)}) copy-start(s32[1,1,32]{2,1,0:T(1,128)} %param.22) | copy-start | bytes 388
  0.7 39.0 %copy-start.16 = (bf16[1,32,4096]{2,1,0:T(8,128)(2,1)S(1)}, bf16[1,32,4096]{2,1,0:T(8,128)(2,1)}, u32[]{:S(2)}) copy-start(bf16[1,32,4096]{2,1,0:T(8,128)(2,1)} %param.19) | copy-start | bytes 786436
  1.8 38.9 %copy-start.17 = (bf16[1,32,4096]{2,1,0:T(8,128)(2,1)S(1)}, bf16[1,32,4096]{2,1,0:T(8,128)(2,1)}, u32[]{:S(2)}) copy-start(bf16[1,32,4096]{2,1,0:T(8,128)(2,1)} %param.20) | copy-start | bytes 786436
  2.6 40.1 %all-to-all-start = ((bf16[32,32,128]{2,0,1:T(8,128)(2,1)}), bf16[32,32,128]{2,0,1:T(8,128)(2,1)S(1)}, u32[]{:S(2)}, u32[]{:S(2)}) async-start(bf16[32,32,128]{2,0,1:T(8,128)(2,1)} %copy.70), calls=%async_computation | async-start | bytes 524288 | tf_op jit(solution)/shard_map/all_to_all | solution.py:112
  12.4 29.9 %collective-permute-start = (f32[1,4096]{1,0:T(1,128)S(1)}, f32[1,4096]{1,0:T(1,128)S(1)}, u32[]{:S(2)}, u32[]{:S(2)}) collective-permute-start(f32[1,4096]{1,0:T(1,128)S(1)} %fusion), channel_id=1, source_target_pairs={{1,0},{2,1},{3,2},{4,3},{5,4},{6,5},{7,6},{8,7},{9,8},{10,9},{11,1... | collective-permute-start | bytes 49160 | tf_op jit(solution)/shard_map/ppermute | solution.py:13
  42.8 19.9 %copy-start.3 = (bf16[32,4096]{1,0:T(8,128)(2,1)}, bf16[32,4096]{1,0:T(8,128)(2,1)S(1)}, u32[]{:S(2)}) copy-start(bf16[32,4096]{1,0:T(8,128)(2,1)S(1)} %add_convert_fusion) | copy-start | bytes 786436
  42.8 14.7 %all-to-all-start.1 = ((bf16[32,32,128]{2,0,1:T(8,128)(2,1)}), bf16[32,32,128]{2,0,1:T(8,128)(2,1)S(1)}, u32[]{:S(2)}, u32[]{:S(2)}) async-start(bf16[32,32,128]{2,0,1:T(8,128)(2,1)} %copy.71), calls=%async_computation.1 | async-start | bytes 524288 | tf_op jit(solution)/shard_map/all_to_all | solution.py:113
  49.3 13.9 %copy-start.14 = (bf16[16,32,1,128]{3,1,0,2:T(8,128)(2,1)}, bf16[16,32,1,128]{3,1,0,2:T(8,128)(2,1)S(1)}, u32[]{:S(2)}) copy-start(bf16[16,32,1,128]{3,1,0,2:T(8,128)(2,1)S(1)} %get-tuple-element.124) | copy-start | bytes 393220
  57.5 5.7 %copy-start.8 = (bf16[32,32,128]{2,0,1:T(8,128)(2,1)}, bf16[32,32,128]{2,0,1:T(8,128)(2,1)S(1)}, u32[]{:S(2)}) copy-start(bf16[32,32,128]{2,0,1:T(8,128)(2,1)S(1)} %all-to-all-done.1) | copy-start | bytes 786436
  57.5 12.8 %all-to-all-start.3 = ((bf16[32,32,128]{2,0,1:T(8,128)(2,1)}), bf16[32,32,128]{2,0,1:T(8,128)(2,1)S(1)}, u32[]{:S(2)}, u32[]{:S(2)}) async-start(bf16[32,32,128]{2,0,1:T(8,128)(2,1)} %copy.73), calls=%async_computation.3 | async-start | bytes 524288 | tf_op jit(solution)/shard_map/all_to_all | solution.py:114
  70.4 13.5 %all-to-all-start.2 = ((bf16[32,32,128]{2,0,1:T(8,128)(2,1)}), bf16[32,32,128]{2,0,1:T(8,128)(2,1)}, u32[]{:S(2)}, u32[]{:S(2)}) async-start(bf16[32,32,128]{2,0,1:T(8,128)(2,1)} %copy_bitcast_fusion), calls=%async_computation.2 | async-start | bytes 524288 | tf_op jit(solution)/shard_map/all_to_all | solution.py:115
  74.8 2.1 copy-start.1
  83.9 3.3 %copy-start.18 = (bf16[16,32,1,128]{3,1,0,2:T(8,128)(2,1)S(1)}, bf16[16,32,1,128]{3,1,0,2:T(8,128)(2,1)}, u32[]{:S(2)}) copy-start(bf16[16,32,1,128]{3,1,0,2:T(8,128)(2,1)} %slice.139) | copy-start | bytes 393220
  85.0 3.4 %copy-start.10 = (bf16[1024,1,128]{2,0,1:T(8,128)(2,1)}, bf16[1024,1,128]{2,0,1:T(8,128)(2,1)S(1)}, u32[]{:S(2)}) copy-start(bf16[1024,1,128]{2,0,1:T(8,128)(2,1)S(1)} %fusion.21) | copy-start | bytes 786436
  87.2 1.8 copy-start.2
  87.5 0.8 copy-start.6
  87.6 1.9 copy-start.9
  89.0 1.6 copy-start.15
  89.5 7.4 %copy-start.7 = (bf16[512,512]{0,1:T(8,128)(2,1)S(1)}, bf16[512,512]{0,1:T(8,128)(2,1)}, u32[]{:S(2)}) copy-start(bf16[512,512]{0,1:T(8,128)(2,1)} %copy-done.6) | copy-start | bytes 1572868
  89.5 7.4 %copy-start.13 = (bf16[16,32,1,128]{3,1,0,2:T(8,128)(2,1)S(1)}, bf16[16,32,1,128]{3,1,0,2:T(8,128)(2,1)}, u32[]{:S(2)}) copy-start(bf16[16,32,1,128]{3,1,0,2:T(8,128)(2,1)} %slice.137) | copy-start | bytes 393220
  92.4 17.3 %copy-start.12 = (bf16[512,128]{1,0:T(8,128)(2,1)S(1)}, bf16[512,128]{1,0:T(8,128)(2,1)}, u32[]{:S(2)}) copy-start(bf16[512,128]{1,0:T(8,128)(2,1)} %convolution_convert_fusion.1) | copy-start | bytes 393220
  93.2 12.8 %all-to-all-start.5 = ((bf16[32,2,2048]{2,1,0:T(2,128)(2,1)}), bf16[32,2,2048]{2,1,0:T(2,128)(2,1)S(1)}, u32[]{:S(2)}, u32[]{:S(2)}) async-start(bf16[32,2,2048]{2,1,0:T(2,128)(2,1)} %reshape.259), calls=%async_computation.5 | async-start | bytes 524288 | tf_op jit(solution)/shard_map/all_to_all | solution.py:140
  97.3 25.9 %copy-start.5 = (bf16[512,512]{0,1:T(8,128)(2,1)S(1)}, bf16[512,512]{0,1:T(8,128)(2,1)}, u32[]{:S(2)}) copy-start(bf16[512,512]{0,1:T(8,128)(2,1)} %fusion.24) | copy-start | bytes 1572868
  97.3 25.9 %copy-start.11 = (bf16[1024,1,128]{2,0,1:T(8,128)(2,1)S(1)}, bf16[1024,1,128]{2,0,1:T(8,128)(2,1)}, u32[]{:S(2)}) copy-start(bf16[1024,1,128]{2,0,1:T(8,128)(2,1)} %copy-done.10) | copy-start | bytes 786436
  106.0 12.8 %all-to-all-start.4 = ((bf16[32,2,2048]{2,1,0:T(2,128)(2,1)}), bf16[32,2,2048]{2,1,0:T(2,128)(2,1)S(1)}, u32[]{:S(2)}, u32[]{:S(2)}) async-start(bf16[32,2,2048]{2,1,0:T(2,128)(2,1)} %reshape.257), calls=%async_computation.4 | async-start | bytes 524288 | tf_op jit(solution)/shard_map/all_to_all | solution.py:137
  118.8 13.5 %all-to-all-start.7 = ((bf16[32,2,2048]{2,1,0:T(2,128)(2,1)}), bf16[32,2,2048]{2,1,0:T(2,128)(2,1)}, u32[]{:S(2)}, u32[]{:S(2)}) async-start(bf16[32,2,2048]{2,1,0:T(2,128)(2,1)} %reshape.263), calls=%async_computation.7 | async-start | bytes 524288 | tf_op jit(solution)/shard_map/all_to_all | solution.py:142
  132.3 91.7 %all-to-all-start.6 = ((bf16[32,2,2048]{2,1,0:T(2,128)(2,1)}), bf16[32,2,2048]{2,1,0:T(2,128)(2,1)}, u32[]{:S(2)}, u32[]{:S(2)}) async-start(bf16[32,2,2048]{2,1,0:T(2,128)(2,1)} %reshape.261), calls=%async_computation.6 | async-start | bytes 524288 | tf_op jit(solution)/shard_map/all_to_all | solution.py:141
  138.5 4.0 %copy-start.4 = (bf16[32,4096]{1,0:T(8,128)(2,1)S(1)}, bf16[32,4096]{1,0:T(8,128)(2,1)}, u32[]{:S(2)}) copy-start(bf16[32,4096]{1,0:T(8,128)(2,1)} %copy-done.3) | copy-start | bytes 786436
where the time goes:
time: 229 us; the launch traced here: 227 us
  blocking collectives  104 us (45%)
  starting transfers between devices  41 us (18%)
  waiting for transfers between devices  31.5 us (14%)
  local copies, waits for them, and re-layouts  22 us (10%)
  other arithmetic  15 us (7%)
  matrix products  11.5 us (5%)
    psum x1, blocking collectives, per_device(): gain_total = lax.psum(seq_terms, ('grp', 'seq'))  80.6 us
    all_gather x1, blocking collectives, per_device(): all_starts = lax.all_gather(seg_starts[0], 'seq', axis=0, tiled=True)  23.7 us
    unnamed x54, local copies, waits for them, and re-layouts  12.4 us
    all_to_all x1, starting transfers between devices, per_device(): lax.all_to_all(by_heads(queries[0]), 'seq', split_axis=1, concat_axis=0,...  8.59 us
    all_to_all x1, waiting for transfers between devices, per_device(): lax.all_to_all(by_heads(attn_keys[0]), 'seq', split_axis=1, concat_axis=0...  8.21 us
    transpose x6, other arithmetic, per_device(): jnp.moveaxis(operand, 0, 1)  8.13 us
    all_to_all x1, starting transfers between devices, per_device(): lax.all_to_all(by_heads(attn_keys[0]), 'seq', split_axis=1, concat_axis=0...  5.75 us
    all_to_all x1, waiting for transfers between devices, per_device(): lax.all_to_all(by_heads(attn_values[0]), 'seq', split_axis=1, concat_axis...  5.39 us
  transfers between devices with their start and end apart: 9, of which 6 were waited for; matrix products, arithmetic and copies ran while one was open for 15% of the time, Pallas kernels for 0%

commit v1 on v0

--- a/solution.py
+++ b/solution.py
@@ -145,7 +145,8 @@
     )
     seq_out = returned[3].reshape(slot_count, model_width)
     seq_terms = jnp.sum(seq_out.astype(jnp.float32) * pooled_low.astype(jnp.float32), axis=0)
-    gain_total = lax.psum(seq_terms, ("grp", "seq"))
+    blocks = lax.all_gather(seq_terms, ("grp", "seq"))
+    gain_total = jnp.sum(blocks, axis=0)
     grad_gain = lax.dynamic_slice_in_dim(gain_total, shard_index * col_count, col_count)
     return (to_seq(returned[0]), to_seq(returned[1]), to_seq(returned[2]), grad_gain)
 

time: 229 us -> 246 us (1.074)
  blocking collectives: 104 us -> 35.3 us
  waiting for transfers between devices: 31.5 us -> 98.7 us
  between operations: 1.82 us -> 15.2 us
  local copies, waits for them, and re-layouts: 22 us -> 27.7 us
  starting transfers between devices: 41 us -> 36.8 us
  matrix products: 11.5 us -> 14.2 us
    psum x1 -> x0, blocking collectives: 80.6 us -> none  [per_device(): gain_total = lax.psum(seq_terms, ('grp', 'seq'))]
    all_gather x0 -> x1, waiting for transfers between devices: none -> 67.2 us  [per_device(): blocks = lax.all_gather(seq_terms, ('grp', 'seq'))]
    all_to_all x0 -> x1, blocking collectives: none -> 13.5 us  [per_device(): lax.all_to_all(shortened(attn_out), 'seq', split_axis=0, concat_axis=1, t...]
    all_to_all x1 -> x0, waiting for transfers between devices: 5.14 us -> none  [per_device(): lax.all_to_all(shortened(attn_out), 'seq', split_axis=0, concat_axis=1, t...]
    all_gather x0 -> x1, local copies, waits for them, and re-layouts: none -> 4.97 us  [per_device(): blocks = lax.all_gather(seq_terms, ('grp', 'seq'))]
    all_to_all x1, waiting for transfers between devices: 0.01 us -> 4.69 us  [per_device(): lax.all_to_all(grad_value, 'seq', split_axis=0, concat_axis=1, tiled=True)]
    all_to_all x1 -> x0, starting transfers between devices: 4.38 us -> none  [per_device(): lax.all_to_all(shortened(attn_out), 'seq', split_axis=0, concat_axis=1, t...]
    all_to_all x1, starting transfers between devices: 8.59 us -> 5.46 us  [per_device(): lax.all_to_all(by_heads(queries[0]), 'seq', split_axis=1, concat_axis=0,...]
  transfers between devices with their start and end apart: 9 -> 9, of which waited for: 6 -> 7; matrix products, arithmetic and copies ran while one was open for 15% -> 14% of each run, Pallas kernels for 0% -> 0%
where the time goes in v1:
time: 246 us; the launch traced here: 245 us
  waiting for transfers between devices  98.7 us (40%)
  starting transfers between devices  36.8 us (15%)
  blocking collectives  35.3 us (14%)
  local copies, waits for them, and re-layouts  27.7 us (11%)
  other arithmetic  17 us (7%)
  between operations  15.2 us (6%)
  matrix products  14.2 us (6%)
    all_gather x1, waiting for transfers between devices, per_device(): blocks = lax.all_gather(seq_terms, ('grp', 'seq'))  67.2 us
    all_gather x1, blocking collectives, per_device(): all_starts = lax.all_gather(seg_starts[0], 'seq', axis=0, tiled=True)  21.8 us
    all_to_all x1, blocking collectives, per_device(): lax.all_to_all(shortened(attn_out), 'seq', split_axis=0, concat_axis=1, t...  13.5 us
    unnamed x52, local copies, waits for them, and re-layouts  13.1 us
    all_to_all x1, waiting for transfers between devices, per_device(): lax.all_to_all(by_heads(attn_keys[0]), 'seq', split_axis=1, concat_axis=0...  8.51 us
    all_to_all x1, waiting for transfers between devices, per_device(): lax.all_to_all(by_heads(attn_values[0]), 'seq', split_axis=1, concat_axis...  7.67 us
    transpose x6, other arithmetic, per_device(): jnp.moveaxis(operand, 0, 1)  7.2 us
    all_to_all x1, starting transfers between devices, per_device(): lax.all_to_all(by_heads(attn_keys[0]), 'seq', split_axis=1, concat_axis=0...  5.46 us
  transfers between devices with their start and end apart: 9, of which 7 were waited for; matrix products, arithmetic and copies ran while one was open for 14% of the time, Pallas kernels for 0%

profile of v1, /device:TPU:1, one launch (start us, length us, event | category | flops | bytes accessed | tf_op | source)
XLA Modules:
  0.0 244.8 jit_solution(1408164344348196173)
XLA Ops:
  9.2 5.1 %collective-permute-start = (f32[1,4096]{1,0:T(1,128)S(1)}, f32[1,4096]{1,0:T(1,128)S(1)}, u32[]{:S(2)}, u32[]{:S(2)}) collective-permute-start(f32[1,4096]{1,0:T(1,128)S(1)} %fusion), channel_id=1, source_target_pairs={{1,0},{2,1},{3,2},{4,3},{5,4},{6,5},{7,6},{8,7},{9,8},{10,9},{11,1... | collective-permute-start | bytes 49160 | tf_op jit(solution)/shard_map/ppermute | solution.py:13
  15.3 5.5 %all-to-all-start = ((bf16[32,32,128]{2,0,1:T(8,128)(2,1)}), bf16[32,32,128]{2,0,1:T(8,128)(2,1)S(1)}, u32[]{:S(2)}, u32[]{:S(2)}) async-start(bf16[32,32,128]{2,0,1:T(8,128)(2,1)} %copy.70), calls=%async_computation | async-start | bytes 524288 | tf_op jit(solution)/shard_map/all_to_all | solution.py:112
  21.4 21.8 %all-gather = s32[32,1,32]{2,1,0:T(1,128)S(1)} all-gather(s32[1,1,32]{2,1,0:T(1,128)S(1)} %copy-done.18), channel_id=2, replica_groups=mesh['grp'=8,'seq'=32] {'seq'}, dimensions={0}, use_global_device_ids=true | all-gather | bytes 4224 | tf_op jit(solution)/shard_map/all_gather | solution.py:104
  46.6 5.5 %all-to-all-start.1 = ((bf16[32,32,128]{2,0,1:T(8,128)(2,1)}), bf16[32,32,128]{2,0,1:T(8,128)(2,1)S(1)}, u32[]{:S(2)}, u32[]{:S(2)}) async-start(bf16[32,32,128]{2,0,1:T(8,128)(2,1)} %copy.71), calls=%async_computation.1 | async-start | bytes 524288 | tf_op jit(solution)/shard_map/all_to_all | solution.py:113
  52.5 8.5 %all-to-all-done.1 = bf16[32,32,128]{2,0,1:T(8,128)(2,1)S(1)} async-done(((bf16[32,32,128]{2,0,1:T(8,128)(2,1)}), bf16[32,32,128]{2,0,1:T(8,128)(2,1)S(1)}, u32[]{:S(2)}, u32[]{:S(2)}) %all-to-all-start.1) | async-done | bytes 262176 | tf_op jit(solution)/shard_map/all_to_all | solution.py:113
  61.1 3.7 %all-to-all-start.3 = ((bf16[32,32,128]{2,0,1:T(8,128)(2,1)}), bf16[32,32,128]{2,0,1:T(8,128)(2,1)S(1)}, u32[]{:S(2)}, u32[]{:S(2)}) async-start(bf16[32,32,128]{2,0,1:T(8,128)(2,1)} %copy.73), calls=%async_computation.3 | async-start | bytes 524288 | tf_op jit(solution)/shard_map/all_to_all | solution.py:114
  66.2 7.7 %all-to-all-done.3 = bf16[32,32,128]{2,0,1:T(8,128)(2,1)S(1)} async-done(((bf16[32,32,128]{2,0,1:T(8,128)(2,1)}), bf16[32,32,128]{2,0,1:T(8,128)(2,1)S(1)}, u32[]{:S(2)}, u32[]{:S(2)}) %all-to-all-start.3) | async-done | bytes 262176 | tf_op jit(solution)/shard_map/all_to_all | solution.py:114
  73.9 4.4 %all-to-all-start.2 = ((bf16[32,32,128]{2,0,1:T(8,128)(2,1)}), bf16[32,32,128]{2,0,1:T(8,128)(2,1)}, u32[]{:S(2)}, u32[]{:S(2)}) async-start(bf16[32,32,128]{2,0,1:T(8,128)(2,1)} %copy_bitcast_fusion), calls=%async_computation.2 | async-start | bytes 524288 | tf_op jit(solution)/shard_map/all_to_all | solution.py:115
  83.8 3.6 %all-to-all-done.2 = bf16[32,32,128]{2,0,1:T(8,128)(2,1)} async-done(((bf16[32,32,128]{2,0,1:T(8,128)(2,1)}), bf16[32,32,128]{2,0,1:T(8,128)(2,1)}, u32[]{:S(2)}, u32[]{:S(2)}) %all-to-all-start.2) | async-done | bytes 262176 | tf_op jit(solution)/shard_map/all_to_all | solution.py:115
  89.2 1.6 multiply_reduce_fusion.1
  92.0 2.4 reduce.19
  94.4 1.7 reshape.264
  96.1 13.5 %all_to_all.108 = bf16[32,2,2048]{2,1,0:T(2,128)(2,1)} all-to-all(bf16[32,2,2048]{2,1,0:T(2,128)(2,1)} %reshape.264), channel_id=1, replica_groups=mesh['grp'=8,'seq'=32] {'seq'}, dimensions={0} | all-to-all | bytes 524288 | tf_op jit(solution)/shard_map/all_to_all | solution.py:142
  109.6 2.8 %reshape.265 = bf16[1024,1,128]{2,1,0:T(2,128)(2,1)} reshape(bf16[32,2,2048]{2,1,0:T(2,128)(2,1)} %all_to_all.108) | data formatting | bytes 524288
  112.4 1.6 convert_element_type.145
  115.4 1.4 fusion.9
  118.6 1.5 reduce.16
  120.1 1.7 reshape.258
  121.8 4.6 %all-to-all-start.4 = ((bf16[32,2,2048]{2,1,0:T(2,128)(2,1)}), bf16[32,2,2048]{2,1,0:T(2,128)(2,1)}, u32[]{:S(2)}, u32[]{:S(2)}) async-start(bf16[32,2,2048]{2,1,0:T(2,128)(2,1)} %reshape.258), calls=%async_computation.4 | async-start | bytes 524288 | tf_op jit(solution)/shard_map/all_to_all | solution.py:137
  126.4 1.4 fusion.34
  127.7 2.1 fusion.13
  129.8 1.8 reduce.17
  132.4 3.0 %all-to-all-done.4 = bf16[32,2,2048]{2,1,0:T(2,128)(2,1)} async-done(((bf16[32,2,2048]{2,1,0:T(2,128)(2,1)}), bf16[32,2,2048]{2,1,0:T(2,128)(2,1)}, u32[]{:S(2)}, u32[]{:S(2)}) %all-to-all-start.4) | async-done | bytes 262176 | tf_op jit(solution)/shard_map/all_to_all | solution.py:137
  135.4 4.3 %all-to-all-start.5 = ((bf16[32,2,2048]{2,1,0:T(2,128)(2,1)}), bf16[32,2,2048]{2,1,0:T(2,128)(2,1)S(1)}, u32[]{:S(2)}, u32[]{:S(2)}) async-start(bf16[32,2,2048]{2,1,0:T(2,128)(2,1)} %reshape.260), calls=%async_computation.5 | async-start | bytes 524288 | tf_op jit(solution)/shard_map/all_to_all | solution.py:140
  141.0 2.1 fusion.14
  144.7 4.0 %all-to-all-done.5 = bf16[32,2,2048]{2,1,0:T(2,128)(2,1)S(1)} async-done(((bf16[32,2,2048]{2,1,0:T(2,128)(2,1)}), bf16[32,2,2048]{2,1,0:T(2,128)(2,1)S(1)}, u32[]{:S(2)}, u32[]{:S(2)}) %all-to-all-start.5) | async-done | bytes 262176 | tf_op jit(solution)/shard_map/all_to_all | solution.py:140
  148.7 3.7 %all-to-all-start.6 = ((bf16[32,2,2048]{2,1,0:T(2,128)(2,1)}), bf16[32,2,2048]{2,1,0:T(2,128)(2,1)S(1)}, u32[]{:S(2)}, u32[]{:S(2)}) async-start(bf16[32,2,2048]{2,1,0:T(2,128)(2,1)} %reshape.262), calls=%async_computation.6 | async-start | bytes 524288 | tf_op jit(solution)/shard_map/all_to_all | solution.py:141
  153.7 2.2 reshape.259
  156.8 4.7 %all-to-all-done.6 = bf16[32,2,2048]{2,1,0:T(2,128)(2,1)S(1)} async-done(((bf16[32,2,2048]{2,1,0:T(2,128)(2,1)}), bf16[32,2,2048]{2,1,0:T(2,128)(2,1)S(1)}, u32[]{:S(2)}, u32[]{:S(2)}) %all-to-all-start.6) | async-done | bytes 262176 | tf_op jit(solution)/shard_map/all_to_all | solution.py:141
  162.8 67.2 %all-gather.4.cloned.1.call-done = f32[1048576]{0:T(1024)} async-done(((f32[4096]{0:T(1024)}), f32[1048576]{0:T(1024)}) %all-gather.4.cloned.1.call-update) | async-done | bytes 4194320 | tf_op jit(solution)/shard_map/all_gather | solution.py:148
  230.0 5.0 %reshape.248 = f32[256,4096]{1,0:T(8,128)} reshape(f32[1048576]{0:T(1024)} %all-gather.4.cloned.1.call-done) | data formatting | bytes 8388608 | tf_op jit(solution)/shard_map/all_gather | solution.py:148
  234.9 2.4 reduce_sum.83
  (99 shorter events, 27.3 us)
Async XLA Ops:
  7.2 1.7 copy-start
  7.2 13.6 %copy-start.18 = (s32[1,1,32]{2,1,0:T(1,128)S(1)}, s32[1,1,32]{2,1,0:T(1,128)}, u32[]{:S(2)}) copy-start(s32[1,1,32]{2,1,0:T(1,128)} %param.22) | copy-start | bytes 388
  7.2 7.2 %copy-start.15 = (bf16[1,32,4096]{2,1,0:T(8,128)(2,1)S(1)}, bf16[1,32,4096]{2,1,0:T(8,128)(2,1)}, u32[]{:S(2)}) copy-start(bf16[1,32,4096]{2,1,0:T(8,128)(2,1)} %param.18) | copy-start | bytes 786436
  7.2 36.9 %copy-start.16 = (bf16[1,32,4096]{2,1,0:T(8,128)(2,1)S(1)}, bf16[1,32,4096]{2,1,0:T(8,128)(2,1)}, u32[]{:S(2)}) copy-start(bf16[1,32,4096]{2,1,0:T(8,128)(2,1)} %param.19) | copy-start | bytes 786436
  8.9 36.1 %copy-start.17 = (bf16[1,32,4096]{2,1,0:T(8,128)(2,1)S(1)}, bf16[1,32,4096]{2,1,0:T(8,128)(2,1)}, u32[]{:S(2)}) copy-start(bf16[1,32,4096]{2,1,0:T(8,128)(2,1)} %param.20) | copy-start | bytes 786436
  9.2 42.8 %collective-permute-start = (f32[1,4096]{1,0:T(1,128)S(1)}, f32[1,4096]{1,0:T(1,128)S(1)}, u32[]{:S(2)}, u32[]{:S(2)}) collective-permute-start(f32[1,4096]{1,0:T(1,128)S(1)} %fusion), channel_id=1, source_target_pairs={{1,0},{2,1},{3,2},{4,3},{5,4},{6,5},{7,6},{8,7},{9,8},{10,9},{11,1... | collective-permute-start | bytes 49160 | tf_op jit(solution)/shard_map/ppermute | solution.py:13
  15.3 31.3 %all-to-all-start = ((bf16[32,32,128]{2,0,1:T(8,128)(2,1)}), bf16[32,32,128]{2,0,1:T(8,128)(2,1)S(1)}, u32[]{:S(2)}, u32[]{:S(2)}) async-start(bf16[32,32,128]{2,0,1:T(8,128)(2,1)} %copy.70), calls=%async_computation | async-start | bytes 524288 | tf_op jit(solution)/shard_map/all_to_all | solution.py:112
  46.6 14.5 %all-to-all-start.1 = ((bf16[32,32,128]{2,0,1:T(8,128)(2,1)}), bf16[32,32,128]{2,0,1:T(8,128)(2,1)S(1)}, u32[]{:S(2)}, u32[]{:S(2)}) async-start(bf16[32,32,128]{2,0,1:T(8,128)(2,1)} %copy.71), calls=%async_computation.1 | async-start | bytes 524288 | tf_op jit(solution)/shard_map/all_to_all | solution.py:113
  52.5 27.2 %copy-start.3 = (bf16[32,4096]{1,0:T(8,128)(2,1)}, bf16[32,4096]{1,0:T(8,128)(2,1)S(1)}, u32[]{:S(2)}) copy-start(bf16[32,4096]{1,0:T(8,128)(2,1)S(1)} %add_convert_fusion) | copy-start | bytes 786436
  61.0 18.7 %copy-start.6 = (bf16[32,32,128]{2,0,1:T(8,128)(2,1)}, bf16[32,32,128]{2,0,1:T(8,128)(2,1)S(1)}, u32[]{:S(2)}) copy-start(bf16[32,32,128]{2,0,1:T(8,128)(2,1)S(1)} %all-to-all-done.1) | copy-start | bytes 786436
  61.1 12.8 %all-to-all-start.3 = ((bf16[32,32,128]{2,0,1:T(8,128)(2,1)}), bf16[32,32,128]{2,0,1:T(8,128)(2,1)S(1)}, u32[]{:S(2)}, u32[]{:S(2)}) async-start(bf16[32,32,128]{2,0,1:T(8,128)(2,1)} %copy.73), calls=%async_computation.3 | async-start | bytes 524288 | tf_op jit(solution)/shard_map/all_to_all | solution.py:114
  66.2 14.1 %copy-start.14 = (bf16[16,32,1,128]{3,1,0,2:T(8,128)(2,1)}, bf16[16,32,1,128]{3,1,0,2:T(8,128)(2,1)S(1)}, u32[]{:S(2)}) copy-start(bf16[16,32,1,128]{3,1,0,2:T(8,128)(2,1)S(1)} %get-tuple-element.124) | copy-start | bytes 393220
  73.9 13.5 %all-to-all-start.2 = ((bf16[32,32,128]{2,0,1:T(8,128)(2,1)}), bf16[32,32,128]{2,0,1:T(8,128)(2,1)}, u32[]{:S(2)}, u32[]{:S(2)}) async-start(bf16[32,32,128]{2,0,1:T(8,128)(2,1)} %copy_bitcast_fusion), calls=%async_computation.2 | async-start | bytes 524288 | tf_op jit(solution)/shard_map/all_to_all | solution.py:115
  78.3 151.7 %all-gather.4.cloned.1.call-start = ((), (), s32[]{:S(2)}) async-start(), calls=%async_computation.8 | async-start | bytes 4210688 | tf_op jit(solution)/shard_map/all_gather | solution.py:148
  80.3 0.9 copy-start.12
  80.8 2.1 copy-start.1
  87.4 3.4 %copy-start.11 = (bf16[512,128]{1,0:T(8,128)(2,1)S(1)}, bf16[512,128]{1,0:T(8,128)(2,1)}, u32[]{:S(2)}) copy-start(bf16[512,128]{1,0:T(8,128)(2,1)} %convolution_convert_fusion.1) | copy-start | bytes 393220
  88.5 0.7 copy-start.8
  112.4 1.9 copy-start.4
  115.3 1.5 copy-start.13
  115.3 2.3 copy-start.2
  115.3 2.3 copy-start.9
  116.8 0.8 copy-start.5
  116.8 1.3 copy-start.7
  121.8 13.6 %all-to-all-start.4 = ((bf16[32,2,2048]{2,1,0:T(2,128)(2,1)}), bf16[32,2,2048]{2,1,0:T(2,128)(2,1)}, u32[]{:S(2)}, u32[]{:S(2)}) async-start(bf16[32,2,2048]{2,1,0:T(2,128)(2,1)} %reshape.258), calls=%async_computation.4 | async-start | bytes 524288 | tf_op jit(solution)/shard_map/all_to_all | solution.py:137
  126.3 13.3 %copy-start.10 = (bf16[1024,1,128]{2,0,1:T(8,128)(2,1)S(1)}, bf16[1024,1,128]{2,0,1:T(8,128)(2,1)}, u32[]{:S(2)}) copy-start(bf16[1024,1,128]{2,0,1:T(8,128)(2,1)} %copy-done.8) | copy-start | bytes 786436
  135.4 13.3 %all-to-all-start.5 = ((bf16[32,2,2048]{2,1,0:T(2,128)(2,1)}), bf16[32,2,2048]{2,1,0:T(2,128)(2,1)S(1)}, u32[]{:S(2)}, u32[]{:S(2)}) async-start(bf16[32,2,2048]{2,1,0:T(2,128)(2,1)} %reshape.260), calls=%async_computation.5 | async-start | bytes 524288 | tf_op jit(solution)/shard_map/all_to_all | solution.py:140
  148.7 12.8 %all-to-all-start.6 = ((bf16[32,2,2048]{2,1,0:T(2,128)(2,1)}), bf16[32,2,2048]{2,1,0:T(2,128)(2,1)S(1)}, u32[]{:S(2)}, u32[]{:S(2)}) async-start(bf16[32,2,2048]{2,1,0:T(2,128)(2,1)} %reshape.262), calls=%async_computation.6 | async-start | bytes 524288 | tf_op jit(solution)/shard_map/all_to_all | solution.py:141
Sparse Core Ops, SparseCore 0:
  115.4 114.4 all-gather.3
